TPU v7x, 32 devices: a whole 2x2x4 slice. The times are simulated.
32 devices in a mesh: tp: 4 (over y, x), dp: 4 (over z), dq: 2 (over core).
Axes of the slice: x: 2, y: 2, z: 4, core: 2. Of those that a mesh axis runs over, the one named last changes fastest.
Arguments:
- inputs: bfloat16 [16384, 768], P(('dp', 'dq')), may hold values from -6 to 6
- token_ids: int32 [64, 256], P(('dp', 'dq')), may hold values from 0 to 30521, as said below
- crop_counts: int32 [8], P(('dp', 'dq')), may hold values from 1 to 8, as said below
- domain_ids: int32 [64], P(('dp', 'dq')), may hold values from 0 to 1
- positives: bfloat16 [64, 768], P(('dp', 'dq')), may hold values from -0.59765625 to 0.59765625
- distractor_buffer: bfloat16 [16384, 768], P(('dp', 'dq')), may hold values from -0.59765625 to 0.59765625
- w_query: bfloat16 [768, 768], P(None, 'tp'), may hold values from -0.21875 to 0.21875
- b_query: float32 [768], P('tp'), may hold values from -1.75 to 1.75
- w_key: bfloat16 [768, 768], P(None, 'tp'), may hold values from -0.21875 to 0.21875
- w_value: bfloat16 [768, 768], P(None, 'tp'), may hold values from -0.21875 to 0.21875
- b_value: float32 [768], P('tp'), may hold values from -1.75 to 1.75
- w_out: bfloat16 [768, 768], P('tp'), may hold values from -2.5 to 2.5
- b_out: float32 [768], replicated, may hold values from -1.75 to 1.75
- gain_one: float32 [768], replicated, may hold values from 0.5 to 1.5
- shift_one: float32 [768], replicated, may hold values from -1.75 to 1.75
- w_up: bfloat16 [768, 3072], P(None, 'tp'), may hold values from -0.21875 to 0.21875
- b_up: float32 [3072], P('tp'), may hold values from -1.75 to 1.75
- w_down: bfloat16 [3072, 768], P('tp'), may hold values from -0.109375 to 0.109375
- b_down: float32 [768], replicated, may hold values from -1.75 to 1.75
- gain_two: float32 [768], replicated, may hold values from 0.5 to 1.5
- shift_two: float32 [768], replicated, may hold values from -1.75 to 1.75
Outputs:
- grad_inputs: float32 [16384, 768], P(('dp', 'dq'))
- grad_w_query: float32 [768, 768], P(None, 'tp')
- grad_b_query: float32 [768], P('tp')
- grad_w_key: float32 [768, 768], P(None, 'tp')
- grad_w_value: float32 [768, 768], P(None, 'tp')
- grad_b_value: float32 [768], P('tp')
- grad_w_out: float32 [768, 768], P('tp')
- grad_b_out: float32 [768], replicated
- grad_gain_one: float32 [768], replicated
- grad_shift_one: float32 [768], replicated
- grad_w_up: float32 [768, 3072], P(None, 'tp')
- grad_b_up: float32 [3072], P('tp')
- grad_w_down: float32 [3072, 768], P('tp')
- grad_b_down: float32 [768], replicated
- grad_gain_two: float32 [768], replicated
- grad_shift_two: float32 [768], replicated
Inputs may be any that keep to these rules, and one draw needn't show every extreme that they name: `token_ids`: each crop holds 64 to 256 nonzero ids as a prefix, then zeros; position 0 holds 101. `crop_counts`: every batch device has at least one live crop; its live crops are its first ones.
All inputs are finite; a program needn't handle non-finite values.
Results may differ from a plain program's by a relative error of at most 0.014.
Values may be sent and summed in bfloat16 or wider, within the bound.
A program may use at most 128 MiB of HBM per device.

v0:
```python
import jax
import jax.numpy as jnp
from jax import lax
from jax.sharding import PartitionSpec as P

HD = 64


ln_eps = 1e-12
logit_divisor = 0.05
loss_scale = 128.0


def combined_all(value, axis, join):
    pieces = jax.tree.map(lambda part: lax.all_gather(part, axis), value)
    head = jax.tree.map(lambda part: part[0], pieces)
    tail = jax.tree.map(lambda part: part[1:], pieces)
    so_far, _ = lax.scan(lambda so_far, piece: (join(so_far, piece), None), head, tail)
    return so_far


def layer_norm(value_in, gain, shift):
    center = jnp.mean(value_in, axis=-1, keepdims=True)
    centered = value_in - center
    variance = jnp.mean(centered * centered, axis=-1, keepdims=True)
    return centered * lax.rsqrt(variance + ln_eps) * gain + shift


def summarize(resid_two, gain_two, shift_two, live_tokens):
    crop_count, seq_len = live_tokens.shape
    output = layer_norm(resid_two, gain_two, shift_two)
    pooled = jnp.sum(output.reshape(crop_count, seq_len, -1) * live_tokens[:, :, None], axis=1)
    pooled = pooled / jnp.sum(live_tokens, axis=1)[:, None]
    return pooled * lax.rsqrt(jnp.sum(pooled * pooled, axis=-1, keepdims=True) + 1e-06)


def merge_max(first_pair, second_pair):
    joint_max = jnp.maximum(first_pair[0], second_pair[0])
    joint_total = first_pair[1] * jnp.exp(first_pair[0] - joint_max) + second_pair[1] * jnp.exp(
        second_pair[0] - joint_max
    )
    return (joint_max, joint_total)


def share_sum(partial_grad):
    owned = lax.psum_scatter(partial_grad, "tp", scatter_dimension=0, tiled=True)
    return lax.all_gather(owned, "tp", axis=0, tiled=True)


def split_heads(rows, crop_count):
    return rows.reshape(crop_count, -1, rows.shape[1] // HD, HD)


def masked_scores(queries, key_rows, keymask):
    scores = (
        jnp.einsum("cqhd,ckhd->chqk", queries, key_rows, preferred_element_type=jnp.float32) * 0.125
    )
    return jnp.where(keymask[:, None, None, :], scores, -1000000000.0)


def forward(
    inputs,
    keymask,
    w_query,
    b_query,
    w_key,
    w_value,
    b_value,
    w_out,
    b_out,
    gain_one,
    shift_one,
    w_up,
    b_up,
    w_down,
    b_down,
):
    crop_count = keymask.shape[0]
    queries = (jnp.dot(inputs, w_query, preferred_element_type=jnp.float32) + b_query).astype(
        jnp.bfloat16
    )
    key_rows = jnp.dot(inputs, w_key, preferred_element_type=jnp.float32).astype(jnp.bfloat16)
    value_rows = (jnp.dot(inputs, w_value, preferred_element_type=jnp.float32) + b_value).astype(
        jnp.bfloat16
    )
    scores = masked_scores(
        split_heads(queries, crop_count), split_heads(key_rows, crop_count), keymask
    )
    row_max = jnp.max(scores, axis=-1, keepdims=True)
    exp_scores = jnp.exp(scores - row_max)
    row_total = jnp.sum(exp_scores, axis=-1, keepdims=True)
    attn_probs = (exp_scores / row_total).astype(jnp.bfloat16)
    log_total = row_max + jnp.log(row_total)
    context = jnp.einsum(
        "chqk,ckhd->cqhd",
        attn_probs,
        split_heads(value_rows, crop_count),
        preferred_element_type=jnp.float32,
    )
    context = context.reshape(inputs.shape[0], -1).astype(jnp.bfloat16)
    attn_partial = jnp.dot(context, w_out, preferred_element_type=jnp.float32)
    attn_out = lax.psum(attn_partial, "tp") + b_out
    resid_one = inputs.astype(jnp.float32) + attn_out
    hidden = layer_norm(resid_one, gain_one, shift_one)
    hidden_low = hidden.astype(jnp.bfloat16)
    pre_gelu = jnp.dot(hidden_low, w_up, preferred_element_type=jnp.float32) + b_up
    active = jax.nn.gelu(pre_gelu, approximate=False).astype(jnp.bfloat16)
    ffn_partial = jnp.dot(active, w_down, preferred_element_type=jnp.float32)
    resid_two = hidden + (lax.psum(ffn_partial, "tp") + b_down)
    return (
        queries,
        key_rows,
        value_rows,
        log_total,
        context,
        resid_one,
        hidden_low,
        pre_gelu,
        active,
        resid_two,
    )


def body(
    inputs,
    token_ids,
    crop_counts,
    domain_ids,
    positives,
    distractor_buffer,
    w_query,
    b_query,
    w_key,
    w_value,
    b_value,
    w_out,
    b_out,
    gain_one,
    shift_one,
    w_up,
    b_up,
    w_down,
    b_down,
    gain_two,
    shift_two,
):
    keymask = token_ids != 0
    live_tokens = keymask.astype(jnp.float32)
    crop_count = token_ids.shape[0]
    batch_groups = lax.axis_size(("dp", "dq"))
    live_crop = (jnp.arange(crop_count, dtype=jnp.int32) < crop_counts[0]).astype(jnp.float32)
    member = (domain_ids[:, None] == jnp.arange(2, dtype=jnp.int32)[None, :]).astype(jnp.float32)
    live_member = (member * live_crop[:, None]).astype(jnp.bfloat16)
    layer_weights = (
        w_query,
        b_query,
        w_key,
        w_value,
        b_value,
        w_out,
        b_out,
        gain_one,
        shift_one,
        w_up,
        b_up,
        w_down,
        b_down,
    )
    forward_kept = forward(inputs, keymask, *layer_weights)
    resid_two = forward_kept[9]

    def pooled_rows(resid_value, gain_value, shift_value):
        return summarize(resid_value, gain_value, shift_value, live_tokens)

    word_vectors, head_back = jax.vjp(pooled_rows, resid_two, gain_two, shift_two)
    embedded_reduced = word_vectors.astype(jnp.bfloat16)
    snippet_gathering, every_member = (
        lax.all_gather(embedded_reduced, ("dp", "dq"), axis=0, tiled=True),
        lax.all_gather(live_member, ("dp", "dq"), axis=0, tiled=True),
    )
    domain_total = jnp.sum(every_member.astype(jnp.float32), axis=0)
    own_total = jnp.sum(member * domain_total[None, :], axis=1)
    crop_weight = (
        loss_scale * live_crop * (crop_count * batch_groups) / (2.0 * jnp.maximum(own_total, 1.0))
    )
    distractor_cosine_scores = (
        jnp.dot(snippet_gathering, distractor_buffer.T, preferred_element_type=jnp.float32)
        / logit_divisor
    )
    local_max = jnp.max(distractor_cosine_scores, axis=-1)
    local_total = jnp.sum(jnp.exp(distractor_cosine_scores - local_max[:, None]), axis=-1)
    merged_max, merged_total = combined_all((local_max, local_total), ("dp", "dq"), merge_max)
    distractor_log_partition = merged_max + jnp.log(merged_total)
    negative_portion = (
        jnp.exp(distractor_cosine_scores - distractor_log_partition[:, None]) / logit_divisor
    )
    share_high = negative_portion.astype(jnp.bfloat16)
    share_rest = (negative_portion - share_high.astype(jnp.float32)).astype(jnp.bfloat16)
    queue_pull = jnp.dot(
        share_high, distractor_buffer, preferred_element_type=jnp.float32
    ) + jnp.dot(share_rest, distractor_buffer, preferred_element_type=jnp.float32)
    pulled = lax.psum_scatter(queue_pull, ("dp", "dq"), scatter_dimension=0, tiled=True)
    own_lse = lax.dynamic_slice_in_dim(
        distractor_log_partition, lax.axis_index(("dp", "dq")) * crop_count, crop_count
    )
    matching_couples = positives.astype(jnp.float32)
    matching_cosine_scores = (
        jnp.sum(embedded_reduced.astype(jnp.float32) * matching_couples, axis=-1) / logit_divisor
    )
    combined_log_partition = jnp.logaddexp(matching_cosine_scores, own_lse)
    grad_embedded = crop_weight[:, None] * (
        jnp.exp(own_lse - combined_log_partition)[:, None] * pulled
        + ((jnp.exp(matching_cosine_scores - combined_log_partition) - 1.0) / logit_divisor)[
            :, None
        ]
        * matching_couples
    )
    grad_resid_two, grad_gain_two, grad_shift_two = head_back(grad_embedded)
    replay_in = lax.optimization_barrier((inputs, grad_resid_two))[0]
    stored = forward(replay_in, keymask, *layer_weights)
    queries, key_rows, value_rows, log_total, context, resid_one, hidden_low, pre_gelu, active = (
        stored[:9]
    )
    grad_b_down = jnp.sum(grad_resid_two, axis=0)
    grad_ffn = grad_resid_two.astype(jnp.bfloat16)
    grad_w_down = jnp.dot(active.T, grad_ffn, preferred_element_type=jnp.float32)
    grad_active = jnp.dot(grad_ffn, w_down.T, preferred_element_type=jnp.float32)
    gelu_back = jax.vjp(lambda value_in: jax.nn.gelu(value_in, approximate=False), pre_gelu)[1]
    grad_pre = gelu_back(grad_active)[0].astype(jnp.bfloat16)
    grad_b_up = jnp.sum(grad_pre.astype(jnp.float32), axis=0)
    grad_w_up = jnp.dot(hidden_low.T, grad_pre, preferred_element_type=jnp.float32)
    grad_hidden = (
        share_sum(jnp.dot(grad_pre, w_up.T, preferred_element_type=jnp.float32)) + grad_resid_two
    )
    norm_back = jax.vjp(layer_norm, resid_one, gain_one, shift_one)[1]
    grad_resid_one, grad_gain_one, grad_shift_one = norm_back(grad_hidden)
    grad_b_out = jnp.sum(grad_resid_one, axis=0)
    grad_attn = grad_resid_one.astype(jnp.bfloat16)
    grad_w_out = jnp.dot(context.T, grad_attn, preferred_element_type=jnp.float32)
    grad_context = jnp.dot(grad_attn, w_out.T, preferred_element_type=jnp.float32).astype(
        jnp.bfloat16
    )
    grad_context = split_heads(grad_context, crop_count)
    query_heads = split_heads(queries, crop_count)
    key_heads = split_heads(key_rows, crop_count)
    value_heads = split_heads(value_rows, crop_count)
    attn_probs = jnp.exp(masked_scores(query_heads, key_heads, keymask) - log_total)
    grad_value = jnp.einsum(
        "chqk,cqhd->ckhd",
        attn_probs.astype(jnp.bfloat16),
        grad_context,
        preferred_element_type=jnp.float32,
    )
    grad_probs = jnp.einsum(
        "cqhd,ckhd->chqk", grad_context, value_heads, preferred_element_type=jnp.float32
    )
    grad_scores = attn_probs * (
        grad_probs - jnp.sum(grad_probs * attn_probs, axis=-1, keepdims=True)
    )
    grad_scores = grad_scores.astype(jnp.bfloat16)
    token_count = inputs.shape[0]
    grad_query = (
        (
            jnp.einsum(
                "chqk,ckhd->cqhd", grad_scores, key_heads, preferred_element_type=jnp.float32
            )
            * 0.125
        )
        .astype(jnp.bfloat16)
        .reshape(token_count, -1)
    )
    grad_key = (
        (
            jnp.einsum(
                "chqk,cqhd->ckhd", grad_scores, query_heads, preferred_element_type=jnp.float32
            )
            * 0.125
        )
        .astype(jnp.bfloat16)
        .reshape(token_count, -1)
    )
    grad_value = grad_value.astype(jnp.bfloat16).reshape(token_count, -1)
    grad_w_query = jnp.dot(inputs.T, grad_query, preferred_element_type=jnp.float32)
    grad_b_query = jnp.sum(grad_query.astype(jnp.float32), axis=0)
    grad_w_key = jnp.dot(inputs.T, grad_key, preferred_element_type=jnp.float32)
    grad_w_value = jnp.dot(inputs.T, grad_value, preferred_element_type=jnp.float32)
    grad_b_value = jnp.sum(grad_value.astype(jnp.float32), axis=0)
    input_part = (
        jnp.dot(grad_query, w_query.T, preferred_element_type=jnp.float32)
        + jnp.dot(grad_key, w_key.T, preferred_element_type=jnp.float32)
        + jnp.dot(grad_value, w_value.T, preferred_element_type=jnp.float32)
    )
    grad_inputs = share_sum(input_part) + grad_resid_one
    summed = tuple(
        lax.psum(
            (
                grad_w_query,
                grad_b_query,
                grad_w_key,
                grad_w_value,
                grad_b_value,
                grad_w_out,
                grad_b_out,
                grad_gain_one,
                grad_shift_one,
                grad_w_up,
                grad_b_up,
                grad_w_down,
                grad_b_down,
                grad_gain_two,
                grad_shift_two,
            ),
            ("dp", "dq"),
        )
    )
    return (grad_inputs,) + summed


def solution(mesh):
    return jax.shard_map(
        body,
        mesh=mesh,
        in_specs=(
            P(("dp", "dq"), None),
            P(("dp", "dq"), None),
            P(("dp", "dq")),
            P(("dp", "dq")),
            P(("dp", "dq"), None),
            P(("dp", "dq"), None),
            P(None, "tp"),
            P("tp"),
            P(None, "tp"),
            P(None, "tp"),
            P("tp"),
            P("tp", None),
            P(),
            P(),
            P(),
            P(None, "tp"),
            P("tp"),
            P("tp", None),
            P(),
            P(),
            P(),
        ),
        out_specs=(
            P(("dp", "dq"), None),
            P(None, "tp"),
            P("tp"),
            P(None, "tp"),
            P(None, "tp"),
            P("tp"),
            P("tp", None),
            P(),
            P(),
            P(),
            P(None, "tp"),
            P("tp"),
            P("tp", None),
            P(),
            P(),
            P(),
        ),
        check_vma=False,
    )
```

profile of v0, /device:TPU:0, one launch (start us, length us, event | category | flops | bytes accessed | tf_op | source)
XLA Modules:
  0.0 1113.1 jit_solution(10606065264602857754)
XLA Ops:
  19.7 3.7 fusion.150
  23.7 141.0 %all-reduce.10.cloned.1.call-done = f32[2048,768]{1,0:T(8,128)} async-done(((f32[2048,768]{1,0:T(8,128)}), f32[2048,768]{1,0:T(8,128)}) %all-reduce.10.cloned.1.call-update) | async-done | bytes 6291472 | tf_op jit(solution)/shard_map/psum | solution.py:102
  164.8 4.8 fusion.139
  172.8 22.7 %fusion.55 = f32[2048,768]{1,0:T(8,128)} fusion(bf16[768,768]{1,0:T(8,128)(2,1)} %param.40, bf16[768,768]{1,0:T(8,128)(2,1)} %param.38, f32[768]{0:T(1024)S(1)} %copy-done.61, f32[768]{0:T(1024)S(1)} %copy-done.49, f32[768]{0:T(1024)S(1)} %copy-done.46, f32[2048]{0:T(1024)S(1)} %add_rsqrt_fusion, f32[2048]{0:T(1024)S(1)} %broadcast_multiply_fusion.2, ...), kind=kOutput, calls=%fused_computation.112 | convolution fusion | flops 4948230144 | bytes 18116608 | tf_op jit(solution)/shard_map/dot_general | solution.py:108
  197.6 12.1 %all-gather.2 = bf16[8,8,2]{1,2,0:T(2,128)(2,1)S(1)} all-gather(bf16[1,8,2]{1,2,0:T(2,128)(2,1)S(1)} %fusion.100), channel_id=1, replica_groups=mesh['tp'=4,'dp'=4,'dq'=2] {'dp','dq'}, dimensions={0}, use_global_device_ids=true | all-gather | bytes 288 | tf_op jit(solution)/shard_map/all_gather | solution.py:179
  210.4 123.8 %all-reduce.12.cloned.1.call-done = f32[2048,768]{1,0:T(8,128)} async-done(((f32[2048,768]{1,0:T(8,128)}), f32[2048,768]{1,0:T(8,128)}) %all-reduce.12.cloned.1.call-update) | async-done | bytes 6291472 | tf_op jit(solution)/shard_map/psum | solution.py:109
  334.2 6.8 fusion.145
  344.1 14.0 %all_gather.25 = bf16[64,768]{1,0:T(8,128)(2,1)S(1)} all-gather(bf16[8,768]{1,0:T(8,128)(2,1)S(1)} %get-tuple-element.92), channel_id=1, replica_groups=mesh['tp'=4,'dp'=4,'dq'=2] {'dp','dq'}, dimensions={0}, use_global_device_ids=true | all-gather | bytes 110592 | tf_op jit(solution)/shard_map/all_gather | solution.py:178
  360.8 16.7 %all-reduce.3 = (f32[512]{0:T(512)S(1)}, f32[512]{0:T(512)S(1)}) all-reduce(f32[512]{0:T(512)S(1)} %dynamic-update-slice, f32[512]{0:T(512)S(1)} %dynamic-update-slice.1), channel_id=2, replica_groups=mesh['tp'=4,'dp'=4,'dq'=2] {'dp','dq'}, use_global_device_ids=true, to_apply=%add | all-reduce | flops 1024 | bytes 8192
  383.2 26.9 %reduce-scatter.4.cloned.1.call-done = f32[8,768]{1,0:T(8,128)} async-done(((f32[64,768]{1,0:T(8,128)}), f32[8,768]{1,0:T(8,128)}) %reduce-scatter.4.cloned.1.call-update) | async-done | bytes 24592 | tf_op jit(solution)/shard_map/reduce_scatter | solution.py:202
  412.7 4.0 fusion.14
  416.7 5.9 fusion.15
  422.7 4.7 fusion.141
  438.3 3.7 fusion.151
  442.3 136.5 %all-reduce.14.cloned.1.call-done = f32[2048,768]{1,0:T(8,128)} async-done(((f32[2048,768]{1,0:T(8,128)}), f32[2048,768]{1,0:T(8,128)}) %all-reduce.14.cloned.1.call-update) | async-done | bytes 6291472 | tf_op jit(solution)/shard_map/psum | solution.py:102
  585.6 17.8 %fusion.9 = (f32[2048,768]{1,0:T(8,128)}, f32[2048,768]{1,0:T(8,128)}) fusion(f32[768]{0:T(1024)S(1)} %copy-done.62, bf16[2048,768]{1,0:T(8,128)(2,1)S(1)} %add_convert_fusion.1, bf16[768,768]{1,0:T(8,128)(2,1)S(1)} %copy-done.60), kind=kOutput, calls=%fused_computation.15 | convolution fusion | flops 2515009536 | bytes 16911360 | tf_op jit(solution)/shard_map/dot_general | solution.py:106
  603.5 8.1 convert_reduce_fusion
  613.3 4.6 fusion.152
  618.0 70.3 %reduce-scatter.6.cloned.1.call-done = f32[512,768]{1,0:T(8,128)} async-done(((f32[2048,768]{1,0:T(8,128)}), f32[512,768]{1,0:T(8,128)}) %reduce-scatter.6.cloned.1.call-update) | async-done | bytes 1572880 | tf_op jit(solution)/shard_map/reduce_scatter | solution.py:46
  688.4 71.9 %all-gather.6.cloned.1.call-done = f32[2048,768]{1,0:T(8,128)} async-done(((f32[512,768]{1,0:T(8,128)}), f32[2048,768]{1,0:T(8,128)}) %all-gather.6.cloned.1.call-update) | async-done | bytes 6291472 | tf_op jit(solution)/shard_map/all_gather | solution.py:47
  760.3 8.1 multiply_reduce_fusion.1
  768.5 4.6 fusion.143
  776.2 4.3 multiply_reduce_fusion.2
  780.5 4.6 multiply_convert_fusion.1
  791.0 3.7 add_add_fusion.2
  794.8 70.3 %reduce-scatter.8.cloned.1.call-done = f32[512,768]{1,0:T(8,128)} async-done(((f32[2048,768]{1,0:T(8,128)}), f32[512,768]{1,0:T(8,128)}) %reduce-scatter.8.cloned.1.call-update) | async-done | bytes 1572880 | tf_op jit(solution)/shard_map/reduce_scatter | solution.py:46
  865.5 6.9 fusion.155
  872.4 12.2 %fusion.37 = f32[768,768]{1,0:T(8,128)} fusion(f32[2048,768]{1,0:T(8,128)} %get-tuple-element.107, f32[2048,768]{1,0:T(8,128)} %get-tuple-element.108, f32[768]{0:T(1024)S(1)} %copy-done.63, f32[2048,768]{1,0:T(8,128)} %get-tuple-element.83), kind=kOutput, calls=%fused_computation.87 | convolution fusion | flops 2423783424 | bytes 21236736 | tf_op jit(solution)/shard_map/dot_general | solution.py:226
  892.1 45.2 %all-gather.8.cloned.1.call-done = f32[2048,768]{1,0:T(8,128)} async-done(((f32[512,768]{1,0:T(8,128)}), f32[2048,768]{1,0:T(8,128)}) %all-gather.8.cloned.1.call-update) | async-done | bytes 6291472 | tf_op jit(solution)/shard_map/all_gather | solution.py:47
  937.3 7.7 add_reduce_fusion
  945.0 30.6 %all-reduce.2 = (f32[192]{0:T(256)}, f32[192]{0:T(256)}, f32[768]{0:T(1024)}, f32[768]{0:T(1024)}, f32[768]{0:T(1024)}, /*index=5*/f32[768]{0:T(1024)}, f32[768]{0:T(1024)}, f32[768]{0:T(1024)}, f32[768]{0:T(1024)}) all-reduce(f32[192]{0:T(256)S(1)} %reduce_sum.340, ...), channel_id=1, replica_groups=mesh['tp'=4,'dp'=4,'dq'=2] {'dp','dq'}, use_global_device_ids=true, to_apply=%region_34.35 | all-reduce | flops 5760 | bytes 46080 | tf_op jit(solution)/shard_map/psum | solution.py:295
  975.6 119.3 %all-reduce.16.cloned.1.call-done = (f32[768,192]{0,1:T(8,128)}, f32[768,192]{0,1:T(8,128)}, f32[768,192]{0,1:T(8,128)}, f32[192,768]{1,0:T(8,128)}, f32[768,768]{1,0:T(8,128)}, /*index=5*/f32[768,768]{1,0:T(8,128)}) async-done(((f32[768,192]{0,1:T(8,128)}, f32[768,192]{0,1:T(8,128)}, f32[768,192]{0,1:T(8,128)}, f32[192,768]{1,0:T(8,128)}, f32[768,768]{1,0:T(8,128)}, /*index=5*/f32[768,768]{1,0:T(8,128)}), ...) | async-done | bytes 7077904 | tf_op jit(solution)/shard_map/psum | solution.py:295
  (282 shorter events, 78.7 us)
Async XLA Ops:
  7.2 351.0 %copy-start = (bf16[2048,768]{1,0:T(8,128)(2,1)S(1)}, bf16[2048,768]{1,0:T(8,128)(2,1)}, u32[]{:S(2)}) copy-start(bf16[2048,768]{1,0:T(8,128)(2,1)} %param.28) | copy-start | bytes 9437188
  7.2 157.5 %all-reduce.10.cloned.1.call-start = ((), (), s32[]{:S(2)}) async-start(), calls=%async_computation.3 | async-start | bytes 12582912 | tf_op jit(solution)/shard_map/psum | solution.py:102
  19.7 145.1 %copy-start.45 = (f32[768]{0:T(1024)S(1)}, f32[768]{0:T(1024)}, u32[]{:S(2)}) copy-start(f32[768]{0:T(1024)} %param.35) | copy-start | bytes 9220
  23.5 310.7 %all-reduce.12.cloned.1.call-start = ((), (), s32[]{:S(2)}) async-start(), calls=%async_computation.4 | async-start | bytes 12582912 | tf_op jit(solution)/shard_map/psum | solution.py:109
  195.5 138.7 %copy-start.53 = (f32[768]{0:T(1024)S(1)}, f32[768]{0:T(1024)}, u32[]{:S(2)}) copy-start(f32[768]{0:T(1024)} %param.41) | copy-start | bytes 9220
  195.5 214.5 %reduce-scatter.4.cloned.1.call-start = ((), (), s32[]{:S(2)}) async-start(), calls=%async_computation.5 | async-start | bytes 221184 | tf_op jit(solution)/shard_map/reduce_scatter | solution.py:202
  196.3 145.7 %copy-start.42 = (f32[8,256]{1,0:T(8,128)}, f32[8,256]{1,0:T(8,128)S(1)}, u32[]{:S(2)}) copy-start(f32[8,256]{1,0:T(8,128)S(1)} %get-tuple-element.99) | copy-start | bytes 24580
  343.9 16.5 %copy-start.58 = (f32[8]{0:T(128)}, f32[8]{0:T(128)S(1)}, u32[]{:S(2)}) copy-start(f32[8]{0:T(128)S(1)} %multiply_reduce_fusion.9) | copy-start | bytes 100
  343.9 16.5 %copy-start.56 = (f32[8]{0:T(128)}, f32[8]{0:T(128)S(1)}, u32[]{:S(2)}) copy-start(f32[8]{0:T(128)S(1)} %add_rsqrt_fusion.1) | copy-start | bytes 100
  360.6 51.0 %copy-start.57 = (f32[8]{0:T(128)S(1)}, f32[8]{0:T(128)}, u32[]{:S(2)}) copy-start(f32[8]{0:T(128)} %copy-done.56) | copy-start | bytes 100
  382.4 196.5 %all-reduce.14.cloned.1.call-start = ((), (), s32[]{:S(2)}) async-start(), calls=%async_computation.6 | async-start | bytes 12582912 | tf_op jit(solution)/shard_map/psum | solution.py:102
  411.7 11.0 slice-start
  412.6 10.0 copy-start.29
  412.6 10.0 slice-start.1
  442.1 246.2 %reduce-scatter.6.cloned.1.call-start = ((), (), s32[]{:S(2)}) async-start(), calls=%async_computation.7 | async-start | bytes 7864320 | tf_op jit(solution)/shard_map/reduce_scatter | solution.py:46
  583.4 20.0 %copy-start.40 = (f32[2048]{0:T(1024)}, f32[2048]{0:T(1024)S(1)}, u32[]{:S(2)}) copy-start(f32[2048]{0:T(1024)S(1)} %multiply_reduce_fusion.4) | copy-start | bytes 24580
  583.5 19.9 %slice-start.6 = ((s8[6291456]{0:T(1024)(128)(4,1)}), s8[4194304]{0:T(1024)(128)(4,1)S(1)}, s32[]{:S(2)}) async-start(s8[6291456]{0:T(1024)(128)(4,1)} %bitcast.174), calls=%async_computation.18 | async-start | bytes 8388608
  585.6 17.8 %copy-start.25 = (bf16[2048,768]{1,0:T(8,128)(2,1)}, bf16[2048,768]{1,0:T(8,128)(2,1)S(1)}, u32[]{:S(2)}) copy-start(bf16[2048,768]{1,0:T(8,128)(2,1)S(1)} %add_convert_fusion.1) | copy-start | bytes 9437188
  585.6 17.8 %slice-start.7 = ((s8[6291456]{0:T(1024)(128)(4,1)}), s8[2097152]{0:T(1024)(128)(4,1)S(1)}, s32[]{:S(2)}) async-start(s8[6291456]{0:T(1024)(128)(4,1)} %bitcast.174), calls=%async_computation.19 | async-start | bytes 4194304
  585.6 17.8 %copy-start.59 = (bf16[768,768]{1,0:T(8,128)(2,1)S(1)}, bf16[768,768]{1,0:T(8,128)(2,1)}, u32[]{:S(2)}) copy-start(bf16[768,768]{1,0:T(8,128)(2,1)} %param.40) | copy-start | bytes 3538948
  617.9 142.4 %all-gather.6.cloned.1.call-start = ((), (), s32[]{:S(2)}) async-start(), calls=%async_computation.8 | async-start | bytes 7864320 | tf_op jit(solution)/shard_map/all_gather | solution.py:47
  688.3 176.8 %reduce-scatter.8.cloned.1.call-start = ((), (), s32[]{:S(2)}) async-start(), calls=%async_computation.9 | async-start | bytes 7864320 | tf_op jit(solution)/shard_map/reduce_scatter | solution.py:46
  688.4 80.1 %copy-start.41 = (f32[2048]{0:T(1024)S(1)}, f32[2048]{0:T(1024)}, u32[]{:S(2)}) copy-start(f32[2048]{0:T(1024)} %copy-done.40) | copy-start | bytes 24580
  688.4 80.1 %copy-start.48 = (f32[768]{0:T(1024)S(1)}, f32[768]{0:T(1024)}, u32[]{:S(2)}) copy-start(f32[768]{0:T(1024)} %param.36) | copy-start | bytes 9220
  794.8 142.5 %all-gather.8.cloned.1.call-start = ((), (), s32[]{:S(2)}) async-start(), calls=%async_computation.10 | async-start | bytes 7864320 | tf_op jit(solution)/shard_map/all_gather | solution.py:47
  865.2 229.7 %all-reduce.16.cloned.1.call-start = ((), (), s32[]{:S(2)}) async-start(), calls=%async_computation.11 | async-start | bytes 14155776 | tf_op jit(solution)/shard_map/psum | solution.py:295
  872.4 12.2 %copy-start.18 = (bf16[24,8,8,256]{3,1,2,0:T(8,128)(2,1)S(1)}, bf16[24,8,8,256]{3,1,2,0:T(8,128)(2,1)}, u32[]{:S(2)}) copy-start(bf16[24,8,8,256]{3,1,2,0:T(8,128)(2,1)} %copy-done.17) | copy-start | bytes 2359300
  872.4 13.9 %copy-start.13 = (bf16[24,8,8,256]{3,1,2,0:T(8,128)(2,1)S(1)}, bf16[24,8,8,256]{3,1,2,0:T(8,128)(2,1)}, u32[]{:S(2)}) copy-start(bf16[24,8,8,256]{3,1,2,0:T(8,128)(2,1)} %copy-done.12) | copy-start | bytes 2359300
  892.1 52.9 %copy-start.51 = (f32[768]{0:T(1024)S(1)}, f32[768]{0:T(1024)}, u32[]{:S(2)}) copy-start(f32[768]{0:T(1024)} %get-tuple-element.50) | copy-start | bytes 9220
  892.1 52.9 %copy-start.52 = (f32[768]{0:T(1024)S(1)}, f32[768]{0:T(1024)}, u32[]{:S(2)}) copy-start(f32[768]{0:T(1024)} %get-tuple-element.82) | copy-start | bytes 9220
  892.1 52.9 %copy-start.55 = (f32[768]{0:T(1024)S(1)}, f32[768]{0:T(1024)}, u32[]{:S(2)}) copy-start(f32[768]{0:T(1024)} %get-tuple-element.115) | copy-start | bytes 9220
  1094.9 11.3 %copy-start.1 = (bf16[2048,768]{1,0:T(8,128)(2,1)S(1)}, bf16[2048,768]{1,0:T(8,128)(2,1)}, u32[]{:S(2)}) copy-start(bf16[2048,768]{1,0:T(8,128)(2,1)} %param.28) | copy-start | bytes 9437188
  (55 other events, 175.0 us)
Sparse Core Ops, SparseCore 0:
  23.6 141.1 all-reduce.9
  195.7 138.4 all-reduce.11
  382.5 27.5 reduce-scatter.3
  442.2 136.5 all-reduce.13
  618.0 70.1 reduce-scatter.5
  690.1 70.1 all-gather.5
  794.9 70.1 reduce-scatter.7
  867.1 70.1 all-gather.7
  941.6 153.2 all-reduce.15
where the time goes:
time: 1120 us; the launch traced here: 1110 us
  waiting for transfers between devices  805 us (72%)
  matrix products  120 us (11%)
  blocking collectives  73.5 us (7%)
  other arithmetic  71 us (6%)
  local copies, waits for them, and re-layouts  24.9 us (2%)
  between operations  16.9 us (2%)
    psum x2, waiting for transfers between devices, forward(): attn_out = lax.psum(attn_partial, 'tp') + b_out  278 us
    reduce_scatter x2, waiting for transfers between devices, share_sum(): lax.psum_scatter(partial_grad, 'tp', scatter_dimension=0, tiled=True)  141 us
    psum x1, waiting for transfers between devices, forward(): resid_two = hidden + (lax.psum(ffn_partial, 'tp') + b_down)  124 us
    psum x1, waiting for transfers between devices, body(): lax.psum((grad_w_query, grad_b_query, grad_w_key, grad_w_value, grad_b_va...  119 us
    all_gather x2, waiting for transfers between devices, share_sum(): return lax.all_gather(owned, 'tp', axis=0, tiled=True)  117 us
    psum x1, blocking collectives, body(): lax.psum((grad_w_query, grad_b_query, grad_w_key, grad_w_value, grad_b_va...  30.6 us
    reduce_scatter x1, waiting for transfers between devices, body(): lax.psum_scatter(queue_pull, ('dp', 'dq'), scatter_dimension=0, tiled=True)  26.9 us
    dot_general x1, matrix products, forward(): ffn_partial = jnp.dot(active, w_down, preferred_element_type=jnp.float32)  22.7 us
  transfers between devices with their start and end apart: 9, of which 9 were waited for; matrix products, arithmetic and copies ran while one was open for 3% of the time, Pallas kernels for 0%

commit v1 on v0

v1 whole, which is shorter than its diff:
```python
import functools

import jax
import jax.numpy as jnp
from jax import lax
from jax.experimental import pallas as pl
from jax.experimental.pallas import tpu as pltpu
from jax.sharding import PartitionSpec as P

HD = 64
LN_EPS = 1e-12
INV_TEMP = 1.0 / 0.05
LOSS_SCALE = 128.0
MASKED = -1000000000.0
BF = jnp.bfloat16
F32 = jnp.float32
MESH = pl.DeviceIdType.MESH


def dot_nn(left, right):
    return lax.dot_general(left, right, (((1,), (0,)), ((), ())), preferred_element_type=F32)


def dot_nt(left, right):
    return lax.dot_general(left, right, (((1,), (1,)), ((), ())), preferred_element_type=F32)


def dot_tn(left, right):
    return lax.dot_general(left, right, (((0,), (0,)), ((), ())), preferred_element_type=F32)


def loop(count, step):
    def run(i, carry):
        step(i)
        return carry

    lax.fori_loop(0, count, run, 0)


def at(index, size):
    return pl.ds(pl.multiple_of(index * size, size), size)


def remote(src, dst, send_sem, recv_sem, device):
    return pltpu.make_async_remote_copy(
        src_ref=src,
        dst_ref=dst,
        send_sem=send_sem,
        recv_sem=recv_sem,
        device_id=device,
        device_id_type=MESH,
    )


def flip(index, bit):
    return index + bit - 2 * bit * lax.rem(index // bit, 2)


def layer_kernel(sizes, *refs):
    tp_n, dp_n, dq_n, crops_dev, seq, width = sizes
    names = (
        "lens", "dom", "cnt", "x_in", "wqkv_in", "wo_in", "wu_in", "wd_in", "queue_in", "bias_in",
        "vec_in", "pos_in",
        "g_out", "dx_out", "vec_out",
        "wqkv", "wo", "wu", "wd", "xb", "qkv", "prob", "ctx", "xh1", "rstd1", "h1b", "act", "gp",
        "r2", "rstd2",
        "x_s", "ctx_s", "h1_s", "act_s", "df_s", "du_s", "do_s", "dqkv_s",
        "df", "du", "do", "dx", "g0", "r_one", "r_two", "z_one", "z_hi", "res",
        "bb", "emsg", "neg", "shares", "pm_out", "pm_in", "xs", "vbuf", "vrecv",
        "loc", "w_ss", "w_rs", "s_ss", "s_rs", "zd_ss", "zd_rs", "b_ss", "b_rs",
        "a_ss", "a_rs", "e_ss", "e_rs", "p_ss", "p_rs",
        "g1_ss", "g1_rs", "g2_ss", "g2_rs", "gz_ss", "gz_rs", "ga_ss", "ga_rs", "gh_ss", "gh_rs",
        "gf_ss", "gf_rs", "x_ss", "x_rs", "v_ss", "v_rs", "out_sem",
    )
    r = dict(zip(names, refs, strict=True))

    class R:
        pass

    k = R()
    for name, ref in r.items():
        setattr(k, name, ref)

    tokens = crops_dev * seq
    groups = dp_n * dq_n
    dp_bits = dp_n.bit_length() - 1
    hi_bits = (dq_n // 2).bit_length() - 1
    heads_w = width // tp_n
    half = width // 2
    head_half = heads_w // 2
    quarter = half // dp_n
    pairs = width // (2 * HD)

    tp, dp, dq = lax.axis_index("tp"), lax.axis_index("dp"), lax.axis_index("dq")
    core = lax.rem(dq, 2)
    t_x = tp + 1 - 2 * lax.rem(tp, 2)
    t_y = lax.rem(tp + 2, 4)
    t_d = 3 - tp
    t_a = t_x + core * (t_y - t_x)
    t_b = t_x + t_y - t_a
    me = dp * dq_n + dq
    dev_a = (t_a, dp, dq)
    dev_b = (t_b, dp, dq)
    dev_s = (tp, dp, dq + 1 - 2 * core)

    def group_dev(g):
        return (tp, g // dq_n, lax.rem(g, dq_n))

    own_half = at(core, half)
    other_half = at(1 - core, half)

    barrier = pltpu.get_barrier_semaphore()
    for t_peer in (t_x, t_y, t_d):
        pl.semaphore_signal(barrier, inc=1, device_id=(t_peer, dp, dq), device_id_type=MESH)

    def greet(i):
        pl.semaphore_signal(
            barrier, inc=1, device_id=group_dev(lax.rem(me + i + 1, groups)), device_id_type=MESH
        )

    loop(groups - 1, greet)

    locals_ = [
        (k.x_in.at[at(tp, tokens)], k.xb),
        (k.wqkv_in.at[0], k.wqkv.at[0, at(tp, heads_w)]),
        (k.wqkv_in.at[1], k.wqkv.at[1, at(tp, heads_w)]),
        (k.wqkv_in.at[2], k.wqkv.at[2, at(tp, heads_w)]),
        (k.wo_in, k.wo.at[at(tp, heads_w)]),
        (k.wu_in, k.wu.at[tp]),
        (k.wd_in, k.wd.at[tp]),
    ] + [(k.queue_in.at[pl.ds(j * tokens, tokens)], k.du.at[j]) for j in range(tp_n)]
    local = [pltpu.make_async_copy(src, dst, k.loc.at[i]) for i, (src, dst) in enumerate(locals_)]
    for copy in local:
        copy.start()
    pl.semaphore_wait(barrier, 3 + groups - 1)

    def part(c, t, h):
        if c < 3:
            return k.wqkv.at[c, pl.ds(pl.multiple_of(t * heads_w + h * head_half, 32), head_half)]
        if c == 3:
            return k.wo.at[pl.ds(pl.multiple_of(t * heads_w + h * head_half, 32), head_half)]
        if c == 4:
            return k.wu.at[t, at(h, half)]
        return k.wd.at[t, pl.ds(pl.multiple_of(h * half + dp * quarter, 16), quarter)]

    def source(c):
        if c < 3:
            return k.wqkv_in.at[c, at(core, head_half)]
        if c == 3:
            return k.wo_in.at[at(core, head_half)]
        if c == 4:
            return k.wu_in.at[at(core, half)]
        return k.wd_in.at[pl.ds(pl.multiple_of(core * half + dp * quarter, 16), quarter)]

    def w_copy(c, i):
        if i == 0:
            return remote(source(c), part(c, tp, core), k.w_ss.at[c, 0], k.w_rs.at[c, 0], dev_a)
        if i == 1:
            return remote(source(c), part(c, tp, core), k.w_ss.at[c, 1], k.w_rs.at[c, 1], dev_b)
        return remote(
            part(c, t_a, core), part(c, t_a, core), k.w_ss.at[c, 2], k.w_rs.at[c, 2], dev_b
        )

    def w_arrived(c, i):
        t = (t_a, t_b, t_d)[i]
        remote(part(c, t, core), part(c, t, core), k.w_ss.at[c, i], k.w_rs.at[c, i], dev_a).wait_recv()

    def s_part(c, t, h):
        return k.wd.at[t, at(h, half)] if c == 5 else part(c, t, h)

    def s_copy(c, i):
        t = (t_a, t_b, t_d)[i]
        return remote(
            s_part(c, t, core), s_part(c, t, core), k.s_ss.at[c, i], k.s_rs.at[c, t], dev_s
        )

    def s_arrived(c, t):
        remote(
            s_part(c, t, 1 - core), s_part(c, t, 1 - core), k.s_ss.at[c, 0], k.s_rs.at[c, t], dev_s
        ).wait_recv()

    def zd_copy(i, j):
        t = (t_a, t_b, t_d)[i]
        return remote(
            part(5, t, core),
            part(5, t, core),
            k.zd_ss.at[i, j],
            k.zd_rs.at[i, dp],
            (tp, lax.rem(dp + 1 + j, dp_n), dq),
        )

    def zd_arrived(i, j):
        t = (t_a, t_b, t_d)[i]
        z = lax.rem(dp + 1 + j, dp_n)
        there = k.wd.at[t, pl.ds(pl.multiple_of(core * half + z * quarter, 16), quarter)]
        remote(there, there, k.zd_ss.at[i, j], k.zd_rs.at[i, z], dev_s).wait_recv()

    def send_own(c):
        w_copy(c, 0).start()
        w_copy(c, 1).start()

    def pass_on(c, sibling=True):
        w_arrived(c, 0)
        w_copy(c, 2).start()
        if sibling:
            s_copy(c, 0).start()
        w_arrived(c, 1)
        if sibling:
            s_copy(c, 1).start()

    def last_on(c):
        w_arrived(c, 2)
        s_copy(c, 2).start()

    bias_peers = (t_x, t_y, t_d)

    def bias_copy(i):
        return remote(
            k.bias_in, k.bb.at[tp], k.b_ss.at[i], k.b_rs.at[i], (bias_peers[i], dp, dq)
        )

    for i in range(3):
        bias_copy(i).start()
    send_own(5)
    send_own(0)
    send_own(1)
    k.bb[tp] = k.bias_in[...]

    pass_on(5, sibling=False)
    for i in range(2):
        for j in range(dp_n - 1):
            zd_copy(i, j).start()
    send_own(2)
    pass_on(0)
    send_own(3)
    pass_on(1)
    send_own(4)
    w_arrived(5, 2)
    for j in range(dp_n - 1):
        zd_copy(2, j).start()
    last_on(0)

    local[0].wait()
    a_copies = [
        remote(k.xb.at[:, other_half], k.x_s, k.a_ss.at[0], k.a_rs.at[0], dev_s),
        remote(k.ctx, k.ctx_s, k.a_ss.at[1], k.a_rs.at[1], dev_s),
        remote(k.h1b, k.h1_s, k.a_ss.at[2], k.a_rs.at[2], dev_s),
    ]
    a_copies[0].start()
    for i in range(3):
        bias_copy(i).wait_recv()

    def project(c):
        local[1 + c].wait()
        for i in range(3):
            s_arrived(c, (t_a, t_b, t_d)[i])

        def tile(i):
            out = dot_nt(k.xb[...], k.wqkv[c, at(i, 256), :])
            if c != 1:
                row = 1 if c == 0 else 2
                bias = k.bb[0, row : row + 1, at(i, 256)]
                for t in range(1, tp_n):
                    bias = bias + k.bb[t, row : row + 1, at(i, 256)]
                out = out + bias
            out = out.astype(BF)
            k.qkv[c, :, at(i, 256)] = out * BF(0.125) if c == 0 else out

        loop(width // 256, tile)

    pass_on(2)
    last_on(1)
    project(0)
    pass_on(3)
    last_on(2)
    project(1)
    project(2)

    lane = lax.broadcasted_iota(jnp.int32, (seq, 2 * HD), 1)
    first_head = lane < HD
    key_lane = lax.broadcasted_iota(jnp.int32, (seq, seq), 1)

    def attend(i):
        crop, pair = i // pairs, lax.rem(i, pairs)
        rows, cols = at(crop, seq), at(pair, 2 * HD)
        live = key_lane < k.lens[crops_dev * tp + crop]
        q, key, val = k.qkv[0, rows, cols], k.qkv[1, rows, cols], k.qkv[2, rows, cols]
        outs = []
        for h in range(2):
            mine = first_head if h == 0 else ~first_head
            s = dot_nt(jnp.where(mine, q, jnp.zeros_like(q)), key)
            s = jnp.where(live, s, MASKED)
            e = jnp.exp(s - jnp.max(s, axis=-1, keepdims=True))
            p = (e / jnp.sum(e, axis=-1, keepdims=True)).astype(BF)
            k.prob[2 * i + h] = p
            outs.append(dot_nn(p, val))
        k.ctx[rows, cols] = jnp.where(first_head, outs[0], outs[1]).astype(BF)

    loop(crops_dev * pairs // 2, attend)
    last_on(3)
    loop(crops_dev * pairs // 2, lambda i: attend(i + crops_dev * pairs // 2))
    a_copies[1].start()

    local[4].wait()
    for i in range(3):
        s_arrived(3, (t_a, t_b, t_d)[i])

    def attn_out(i):
        rows = at(i, 256)
        k.r2[rows, :] = (
            dot_nn(k.ctx[rows, :], k.wo[...]) + k.vec_in[0:1, :] + k.xb[rows, :].astype(F32)
        )

    loop(tokens // 256, attn_out)

    def norm(v):
        centered = v - jnp.mean(v, axis=-1, keepdims=True)
        rstd = lax.rsqrt(jnp.mean(centered * centered, axis=-1, keepdims=True) + LN_EPS)
        return centered * rstd, rstd

    def norm_one(i):
        rows = at(i, 64)
        xh, rstd = norm(k.r2[rows, :])
        k.xh1[rows, :] = xh
        k.rstd1[rows, :] = rstd
        h1 = xh * k.vec_in[1:2, :] + k.vec_in[2:3, :]
        k.h1b[rows, :] = h1.astype(BF)
        k.r2[rows, :] = h1 + k.vec_in[3:4, :]

    loop(tokens // 64, norm_one)
    a_copies[2].start()

    def act_copy(i):
        t = (tp, t_a, t_b, t_d)[i]
        return remote(
            k.act.at[t, :, other_half], k.act_s.at[t], k.a_ss.at[3 + i], k.a_rs.at[3 + t], dev_s
        )

    def up(t):
        def tile(i):
            cols = at(i, 256)
            u = dot_nn(k.h1b[...], k.wu[t, :, cols]) + k.bb[t, 0:1, cols]
            cdf = 0.5 * lax.erf(u * 0.7071067811865476) + 0.5
            k.act[t, :, cols] = (u * cdf).astype(BF)
            k.gp[t, :, cols] = (cdf + u * (jnp.exp(u * u * -0.5) * 0.3989422804014327)).astype(BF)

        loop(width // 256, tile)

    def down(t):
        def tile(i):
            cols = at(i, 256)
            k.r2[:, cols] += dot_nn(k.act[t], k.wd[t, :, cols])

        loop(width // 256, tile)

    local[5].wait()
    local[6].wait()
    up(tp)
    act_copy(0).start()
    pass_on(4)
    for i in range(3):
        for j in range(dp_n - 1):
            zd_arrived(i, j)
        s_copy(5, i).start()
    down(tp)
    s_arrived(4, t_a)
    up(t_a)
    act_copy(1).start()
    s_arrived(4, t_b)
    up(t_b)
    act_copy(2).start()
    s_arrived(5, t_a)
    down(t_a)
    s_arrived(5, t_b)
    down(t_b)
    last_on(4)
    s_arrived(5, t_d)
    s_arrived(4, t_d)
    up(t_d)
    act_copy(3).start()
    down(t_d)

    sub64 = lax.broadcasted_iota(jnp.int32, (64, 1), 0)
    zero_row = jnp.zeros((1, width), F32)
    lens_f = [k.lens[crops_dev * tp + c].astype(F32) for c in range(crops_dev)]
    k.xs[...] = jnp.zeros_like(k.xs)
    for c in range(crops_dev):

        def norm_two(i, total, c=c):
            rows = pl.ds(pl.multiple_of(c * seq + i * 64, 64), 64)
            xh, rstd = norm(k.r2[rows, :])
            k.r2[rows, :] = xh
            k.rstd2[rows, :] = rstd
            live = sub64 + i * 64 < k.lens[crops_dev * tp + c]
            return total + jnp.sum(jnp.where(live, xh, 0.0), axis=0, keepdims=True)

        k.xs[c : c + 1, :] = lax.fori_loop(0, seq // 64, norm_two, zero_row)

    row8 = lax.broadcasted_iota(jnp.int32, (8, 1), 0)
    row8w = lax.broadcasted_iota(jnp.int32, (8, width), 0)
    lane8w = lax.broadcasted_iota(jnp.int32, (8, width), 1)

    def per_crop(values, other=0.0):
        out = jnp.full((8, 1), other, F32)
        for c in range(crops_dev):
            out = jnp.where(row8 == c, values[c], out)
        return out

    crop_len = per_crop(lens_f, 1.0)
    gain_two, shift_two = k.vec_in[4:5, :], k.vec_in[5:6, :]
    xs = k.xs[...]
    is_crop = row8 < crops_dev
    pooled = jnp.where(is_crop, xs / crop_len * gain_two + shift_two, 0.0)
    inv_norm = lax.rsqrt(jnp.sum(pooled * pooled, axis=-1, keepdims=True) + 1e-06)
    e_own = (pooled * inv_norm).astype(BF).astype(F32)
    live_n = k.cnt[0]
    crops_group = crops_dev * tp_n
    dom_total = [jnp.float32(0.0), jnp.float32(0.0)]
    for c in range(crops_group):
        is_live = jnp.where(c < live_n, 1.0, 0.0)
        is_one = k.dom[c].astype(F32)
        dom_total[0] = dom_total[0] + is_live * (1.0 - is_one)
        dom_total[1] = dom_total[1] + is_live * is_one
    meta = jnp.where(lane8w == 0, dom_total[0], jnp.where(lane8w == 1, dom_total[1], 0.0))
    k.emsg[me] = jnp.where(row8w == crops_dev, meta, e_own)

    def e_copy(i):
        return remote(
            k.emsg.at[me],
            k.emsg.at[me],
            k.e_ss.at[i],
            k.e_rs.at[me],
            group_dev(lax.rem(me + 1 + i, groups)),
        )

    def e_wait(i):
        g = lax.rem(me + 1 + i, groups)
        remote(k.emsg.at[g], k.emsg.at[g], k.e_ss.at[i], k.e_rs.at[g], dev_s).wait_recv()

    loop(groups - 1, lambda i: e_copy(i).start())
    for copy in local[7:]:
        copy.wait()
    loop(groups - 1, e_wait)

    row64 = lax.rem(lax.broadcasted_iota(jnp.int32, (64, 1), 0), 8)
    n_block = 8

    def queue_block(b):
        es = k.emsg[pl.ds(b * n_block, n_block)].reshape(64, width)
        es = jnp.where(row64 < crops_dev, es, 0.0).astype(BF)
        for j in range(tp_n):
            k.neg[:, j * tokens : (j + 1) * tokens] = dot_nt(es, k.du[j]) * INV_TEMP
        neg = k.neg[...]
        top = jnp.max(neg, axis=-1, keepdims=True)
        share = jnp.exp(neg - top)
        total = jnp.sum(share, axis=-1, keepdims=True)
        high = share.astype(BF)
        k.shares[0:64, :] = high
        k.shares[64:128, :] = (share - high.astype(F32)).astype(BF)

        def pull(i):
            cols = at(i, 256)
            both = dot_nn(k.shares[:, 0:tokens], k.du[0, :, cols])
            for j in range(1, tp_n):
                both = both + dot_nn(k.shares[:, j * tokens : (j + 1) * tokens], k.du[j, :, cols])
            k.pm_out[pl.ds(b * n_block, n_block), :, cols] = (both[0:64] + both[64:128]).reshape(
                n_block, 8, 256
            )

        loop(width // 256, pull)
        first = lax.broadcasted_iota(jnp.int32, (64, 128), 1) == 0
        k.pm_out[pl.ds(b * n_block, n_block), :, width:] = jnp.where(first, top, total).reshape(
            n_block, 8, 128
        )

    loop(groups // n_block, queue_block)

    def p_copy(i):
        g = lax.rem(me + 1 + i, groups)
        return remote(k.pm_out.at[g], k.pm_in.at[me], k.p_ss.at[i], k.p_rs.at[me], group_dev(g))

    def p_wait(i):
        g = lax.rem(me + 1 + i, groups)
        remote(k.pm_in.at[g], k.pm_in.at[g], k.p_ss.at[i], k.p_rs.at[g], dev_s).wait_recv()

    loop(groups - 1, lambda i: p_copy(i).start())
    k.pm_in[me] = k.pm_out[me]
    loop(groups - 1, p_wait)

    tops = k.pm_in[:, :, width:]
    top_all = jnp.max(tops, axis=0)[:, 0:1]
    dom_lanes = jnp.sum(k.emsg[:, crops_dev : crops_dev + 1, 0:128], axis=0)

    def merge(g, carry):
        total, pulled = carry
        stats = k.pm_in[g, :, width:]
        scale = jnp.exp(stats[:, 0:1] - top_all)
        return (total + scale * stats[:, 1:2], pulled + scale * k.pm_in[g, :, 0:width])

    total_all, pulled = lax.fori_loop(
        0, groups, merge, (jnp.zeros((8, 1), F32), jnp.zeros((8, width), F32))
    )
    lse_q = top_all + jnp.log(total_all)
    positives = k.pos_in[...]
    pos = jnp.sum(e_own * positives, axis=-1, keepdims=True) * INV_TEMP
    top_both = jnp.maximum(pos, lse_q)
    lse = top_both + jnp.log(jnp.exp(pos - top_both) + jnp.exp(lse_q - top_both))
    weights = []
    for c in range(crops_dev):
        at_c = crops_dev * tp + c
        is_one = k.dom[at_c].astype(F32)
        own_total = dom_lanes[:, 0:1] * (1.0 - is_one) + dom_lanes[:, 1:2] * is_one
        is_live = jnp.where(at_c < live_n, 1.0, 0.0)
        weights.append(
            is_live * (LOSS_SCALE * crops_group * groups) / (2.0 * jnp.maximum(own_total, 1.0))
        )
    crop_weight = per_crop(weights)
    de = crop_weight * (
        (jnp.exp(lse_q - lse) / total_all * INV_TEMP) * pulled
        + ((jnp.exp(pos - lse) - 1.0) * INV_TEMP) * positives
    )
    dpool = inv_norm * (de - pooled * (jnp.sum(pooled * de, axis=-1, keepdims=True) * inv_norm * inv_norm))
    dpool = jnp.where(is_crop, dpool / crop_len, 0.0)
    vec = k.vbuf.at[0]
    vec[...] = jnp.zeros_like(vec)
    vec[6:7, :] = jnp.sum(dpool * xs, axis=0, keepdims=True)
    vec[7:8, :] = jnp.sum(dpool * crop_len, axis=0, keepdims=True)

    dgain = dpool * gain_two
    dgain_mean = jnp.mean(dgain, axis=-1, keepdims=True)
    b_down_sum = zero_row
    for c in range(crops_dev):
        dg, dg_mean = dgain[c : c + 1, :], dgain_mean[c : c + 1, :]

        def norm_two_back(i, total, c=c, dg=dg, dg_mean=dg_mean):
            rows = pl.ds(pl.multiple_of(c * seq + i * 64, 64), 64)
            xh = k.r2[rows, :]
            live = sub64 + i * 64 < k.lens[crops_dev * tp + c]
            scale = jnp.where(live, k.rstd2[rows, :], 0.0)
            dr = scale * (dg - dg_mean - xh * jnp.mean(dg * xh, axis=-1, keepdims=True))
            k.r2[rows, :] = dr
            k.df[rows, :] = dr.astype(BF)
            return total + jnp.sum(dr, axis=0, keepdims=True)

        b_down_sum = lax.fori_loop(0, seq // 64, norm_two_back, b_down_sum)
    vec[3:4, :] = b_down_sum
    df_copy = remote(k.df, k.df_s, k.a_ss.at[7], k.a_rs.at[7], dev_s)
    df_copy.start()

    for c in range(6):
        for i in range(3):
            w_copy(c, i).wait_send()
            s_copy(c, i).wait_send()
    for i in range(3):
        for j in range(dp_n - 1):
            zd_copy(i, j).wait_send()
        bias_copy(i).wait_send()
    for i in range(4):
        act_copy(i).wait_send()
    for copy in a_copies:
        copy.wait_send()
    loop(groups - 1, lambda i: e_copy(i).wait_send())
    loop(groups - 1, lambda i: p_copy(i).wait_send())

    g_ref = (lambda t: k.g0.at[t], lambda t: k.act.at[t, 0:half], lambda t: k.gp.at[t, 0:half])

    def g1_copy(n, i):
        t_from, t_to = ((t_a, 0), (t_d, 1))[i]
        return remote(g_ref[n](t_from), k.r_one.at[n, t_to], k.g1_ss.at[n, i], k.g1_rs.at[n, i], dev_a)

    def g2_copy(n):
        return remote(g_ref[n](t_b), k.r_two.at[n], k.g2_ss.at[n], k.g2_rs.at[n], dev_b)

    def z_span(bits):
        start, size = 0, half
        for bit in range(bits):
            size //= 2
            start = start + lax.rem(dp // (1 << bit), 2) * size
        return start, size

    def z_dev(bit):
        return (tp, flip(dp, 1 << bit), dq)

    def z_rows(start, size):
        return pl.ds(pl.multiple_of(start, 16), size)

    def gz_copy(n, bit):
        start, size = z_span(bit)
        size //= 2
        away = start + (1 - lax.rem(dp // (1 << bit), 2)) * size
        offset = half - 2 * size
        return remote(
            g_ref[n](tp).at[z_rows(away, size)],
            k.z_one.at[n, pl.ds(offset, size)],
            k.gz_ss.at[n, bit],
            k.gz_rs.at[n, bit],
            z_dev(bit),
        )

    def gz_add(n, bit):
        start, size = z_span(bit + 1)
        offset = half - 2 * size
        mine = g_ref[n](tp).at[z_rows(start, size)]
        total = mine[...].astype(F32) + k.z_one[n, pl.ds(offset, size)].astype(F32)
        if bit == dp_bits - 1 and hi_bits == 0:
            k.res[n, z_rows(start, size)] = total.astype(BF)
        else:
            mine[...] = total.astype(BF)

    def gh_copy(n, bit):
        start, size = z_span(dp_bits)
        return remote(
            g_ref[n](tp).at[z_rows(start, size)],
            k.z_hi.at[n, bit],
            k.gh_ss.at[n, bit],
            k.gh_rs.at[n, bit],
            (tp, dp, flip(dq, 2 << bit)),
        )

    def ga_copy(n, bit):
        start, size = z_span(bit + 1)
        rows = k.res.at[n, z_rows(start, size)]
        return remote(rows, rows, k.ga_ss.at[n, bit], k.ga_rs.at[n, bit], z_dev(bit))

    def ga_wait(n, bit):
        start, size = z_span(bit)
        away = start + (1 - lax.rem(dp // (1 << bit), 2)) * (size // 2)
        rows = k.res.at[n, z_rows(away, size // 2)]
        remote(rows, rows, k.ga_ss.at[n, bit], k.ga_rs.at[n, bit], dev_s).wait_recv()

    def gf_copy(n):
        dst = k.g_out.at[n, own_half]
        return remote(k.res.at[n], dst, k.gf_ss.at[n], k.gf_rs.at[n], dev_s)

    def gf_local(n):
        return pltpu.make_async_copy(k.res.at[n], k.g_out.at[n, own_half], k.out_sem.at[n])

    def add_rows(dst, src):
        def step(i):
            rows = at(i, 64)
            dst[rows, :] = (dst[rows, :].astype(F32) + src[rows, :].astype(F32)).astype(BF)

        loop(half // 64, step)

    def plane_first(n):
        g1_copy(n, 0).start()
        g1_copy(n, 1).start()

    def plane_second(n):
        g1_copy(n, 1).wait_recv()
        add_rows(g_ref[n](t_b), k.r_one.at[n, 1])
        g2_copy(n).start()
        g1_copy(n, 0).wait_recv()
        add_rows(g_ref[n](tp), k.r_one.at[n, 0])

    def plane_done(n):
        g2_copy(n).wait_recv()
        add_rows(g_ref[n](tp), k.r_two.at[n])
        gz_copy(n, 0).start()

    def z_step(n, bit):
        gz_copy(n, bit).wait_recv()
        gz_copy(n, bit).wait_send()
        gz_add(n, bit)
        if bit + 1 < dp_bits:
            gz_copy(n, bit + 1).start()

    def z_finish_reduce(n):
        for bit in range(hi_bits):
            gh_copy(n, bit).start()
            gh_copy(n, bit).wait()
            start, size = z_span(dp_bits)
            mine = g_ref[n](tp).at[z_rows(start, size)]
            total = (mine[...].astype(F32) + k.z_hi[n, bit].astype(F32)).astype(BF)
            if bit == hi_bits - 1:
                k.res[n, z_rows(start, size)] = total
            else:
                mine[...] = total
        ga_copy(n, dp_bits - 1).start()

    def z_back(n, bit):
        ga_wait(n, bit)
        if bit > 0:
            ga_copy(n, bit - 1).start()
        else:
            gf_copy(n).start()
            gf_local(n).start()

    def du_copy(i):
        t = (tp, t_a, t_b, t_d)[i]
        return remote(
            k.du.at[t, :, other_half], k.du_s.at[t], k.a_ss.at[8 + i], k.a_rs.at[8 + t], dev_s
        )

    def hidden_back(t):
        def tile(i, _):
            cols = at(i, 256)
            da = dot_nt(k.df[...], k.wd[t, cols, :])
            d = (da * k.gp[t, :, cols].astype(F32)).astype(BF)
            k.du[t, :, cols] = d
            vec[pl.ds(8 + t, 1), cols] = jnp.sum(d.astype(F32), axis=0, keepdims=True)
            return _

        lax.fori_loop(0, width // 256, tile, 0)

    def down_piece(t):
        k.g0[t] = (
            dot_tn(k.act[t, :, own_half], k.df[...]) + dot_tn(k.act_s[t], k.df_s[...])
        ).astype(BF)

    def up_piece(t):
        for h in range(2):
            rows = slice(h * half, (h + 1) * half)
            k.act[t, 0:half, rows] = (
                dot_tn(k.h1b[:, rows], k.du[t, :, own_half]) + dot_tn(k.h1_s[:, rows], k.du_s[t])
            ).astype(BF)

    hidden_back(t_a)
    du_copy(1).start()
    df_copy.wait()
    for t in range(tp_n):
        remote(k.act_s.at[t], k.act_s.at[t], k.a_ss.at[3], k.a_rs.at[3 + t], dev_s).wait_recv()
    down_piece(t_a)
    down_piece(t_d)
    plane_first(0)
    down_piece(t_b)
    down_piece(tp)
    hidden_back(t_d)
    du_copy(3).start()
    hidden_back(t_b)
    du_copy(2).start()
    hidden_back(tp)
    du_copy(0).start()
    a_copies[2].wait_recv()

    def du_arrived(t):
        remote(k.du_s.at[t], k.du_s.at[t], k.a_ss.at[8], k.a_rs.at[8 + t], dev_s).wait_recv()

    du_arrived(t_a)
    up_piece(t_a)
    du_arrived(t_d)
    up_piece(t_d)
    plane_first(1)
    plane_second(0)
    du_arrived(t_b)
    up_piece(t_b)
    du_arrived(tp)
    up_piece(tp)

    def hidden_grad(i):
        cols = at(i, 256)
        total = k.r2[:, cols]
        for t in range(tp_n):
            total = total + dot_nt(k.du[t], k.wu[t, cols, :])
        k.r2[:, cols] = total

    loop(width // 256, hidden_grad)

    gain_one = k.vec_in[1:2, :]

    def norm_one_back(i, sums):
        rows = at(i, 64)
        dh, xh = k.r2[rows, :], k.xh1[rows, :]
        dxh = dh * gain_one
        dr = k.rstd1[rows, :] * (
            dxh
            - jnp.mean(dxh, axis=-1, keepdims=True)
            - xh * jnp.mean(dxh * xh, axis=-1, keepdims=True)
        )
        k.r2[rows, :] = dr
        k.do[rows, :] = dr.astype(BF)
        return (
            sums[0] + jnp.sum(dr, axis=0, keepdims=True),
            sums[1] + jnp.sum(dh * xh, axis=0, keepdims=True),
            sums[2] + jnp.sum(dh, axis=0, keepdims=True),
        )

    out_sum, gain_sum, shift_sum = lax.fori_loop(
        0, tokens // 64, norm_one_back, (zero_row, zero_row, zero_row)
    )
    vec[2:3, :] = out_sum
    vec[4:5, :] = gain_sum
    vec[5:6, :] = shift_sum
    do_copy = remote(k.do.at[:, other_half], k.do_s, k.a_ss.at[12], k.a_rs.at[12], dev_s)
    do_copy.start()

    def context_grad(i):
        k.df[:, at(i, 256)] = dot_nt(k.do[...], k.wo[at(i, 256), :]).astype(BF)

    loop(width // 256, context_grad)
    plane_done(0)

    dqkv = [k.wd.at[c, 0:tokens] for c in range(3)]

    def attend_back(i):
        crop, pair = i // pairs, lax.rem(i, pairs)
        rows, cols = at(crop, seq), at(pair, 2 * HD)
        q, key, val = k.qkv[0, rows, cols], k.qkv[1, rows, cols], k.qkv[2, rows, cols]
        dctx = k.df[rows, cols]
        dqs, dks, dvs = [], [], []
        for h in range(2):
            mine = first_head if h == 0 else ~first_head
            p = k.prob[2 * i + h]
            pf = p.astype(F32)
            dprob = dot_nt(jnp.where(mine, dctx, jnp.zeros_like(dctx)), val)
            ds = (pf * (dprob - jnp.sum(dprob * pf, axis=-1, keepdims=True))).astype(BF)
            dvs.append(dot_tn(p, dctx))
            dqs.append(dot_nn(ds, key))
            dks.append(dot_tn(ds, q))
        dqkv[0][rows, cols] = (jnp.where(first_head, dqs[0], dqs[1]) * 0.125).astype(BF)
        dqkv[1][rows, cols] = jnp.where(first_head, dks[0], dks[1]).astype(BF)
        dqkv[2][rows, cols] = jnp.where(first_head, dvs[0], dvs[1]).astype(BF)

    n_att = crops_dev * pairs
    loop(n_att // 2, attend_back)
    z_step(0, 0)
    plane_second(1)
    loop(n_att // 2, lambda i: attend_back(i + n_att // 2))

    dqkv_copies = [
        remote(dqkv[c], k.dqkv_s.at[c], k.a_ss.at[13 + c], k.a_rs.at[13 + c], dev_s)
        for c in range(3)
    ]
    for copy in dqkv_copies:
        copy.start()
    for bit in range(1, dp_bits):
        z_step(0, bit)
    z_finish_reduce(0)

    def input_grad(i):
        cols = at(i, 256)
        total = k.r2[:, cols]
        for c in range(3):
            total = total + dot_nn(dqkv[c][...], k.wqkv[c, :, cols])
        k.dx[:, cols] = total.astype(BF)

    spots = ((0, 0), (0, 1), (1, 0), (1, 1))

    def head_pieces(c):
        row, col = spots[c]

        def step(i):
            cols = at(i, half)
            if c < 3:
                g = dot_tn(dqkv[c][:, cols], k.xb[:, own_half]) + dot_tn(
                    k.dqkv_s[c, :, cols], k.x_s[...]
                )
            else:
                g = dot_tn(k.ctx[:, cols], k.do[:, own_half]) + dot_tn(k.ctx_s[:, cols], k.do_s[...])
            g = g.astype(BF)
            span = slice(row * heads_w, (row + 1) * heads_w)
            lanes = slice(col * half, (col + 1) * half)
            k.gp[2 * i, span, lanes] = g[0:heads_w]
            k.gp[2 * i + 1, span, lanes] = g[heads_w:]

        loop(tp_n // 2, step)

    a_copies[0].wait_recv()
    a_copies[1].wait_recv()
    do_copy.wait()
    head_pieces(3)
    for c in range(3):
        dqkv_copies[c].wait()
        head_pieces(c)
    plane_first(2)
    vec[0:1, :] = jnp.sum(dqkv[0][...].astype(F32), axis=0, keepdims=True)
    vec[1:2, :] = jnp.sum(dqkv[2][...].astype(F32), axis=0, keepdims=True)
    plane_done(1)
    loop(width // 256, input_grad)

    def dx_rows(t):
        return k.dx_out.at[at(t, tokens)]

    def dx_copy(i):
        if i == 0:
            return remote(k.dx, dx_rows(tp), k.x_ss.at[0], k.x_rs.at[0], dev_a)
        if i == 1:
            return remote(k.dx, dx_rows(tp), k.x_ss.at[1], k.x_rs.at[1], dev_b)
        return remote(dx_rows(t_a), dx_rows(t_a), k.x_ss.at[2], k.x_rs.at[2], dev_b)

    def dx_arrived(i):
        there = dx_rows((t_a, t_b, t_d)[i])
        remote(there, there, k.x_ss.at[i], k.x_rs.at[i], dev_a).wait_recv()

    dx_copy(0).start()
    dx_copy(1).start()
    dx_local = pltpu.make_async_copy(k.dx, dx_rows(tp), k.out_sem.at[3])
    dx_local.start()

    rounds = (
        [dev_s, (t_x, dp, dq), (t_y, dp, dq)]
        + [z_dev(bit) for bit in range(dp_bits)]
        + [(tp, dp, flip(dq, 2 << bit)) for bit in range(hi_bits)]
    )

    def v_copy(i):
        return remote(k.vbuf.at[i], k.vrecv.at[i], k.v_ss.at[i], k.v_rs.at[i], rounds[i])

    def v_step(i):
        v_copy(i).wait_recv()
        k.vbuf[i + 1] = k.vbuf[i] + k.vrecv[i]
        if i + 1 < len(rounds):
            v_copy(i + 1).start()

    v_copy(0).start()
    for bit in range(dp_bits - 1, 0, -1):
        z_back(0, bit)
    z_step(1, 0)
    v_step(0)
    plane_second(2)
    z_back(0, 0)
    for bit in range(1, dp_bits):
        z_step(1, bit)
    z_finish_reduce(1)
    v_step(1)
    for bit in range(dp_bits - 1, -1, -1):
        z_back(1, bit)
    v_step(2)
    plane_done(2)
    dx_arrived(0)
    dx_copy(2).start()
    for bit in range(dp_bits):
        z_step(2, bit)
    z_finish_reduce(2)
    for bit in range(dp_bits - 1, -1, -1):
        z_back(2, bit)
    for i in range(3, len(rounds)):
        v_step(i)
    k.vec_out[...] = k.vbuf[len(rounds)]

    dx_arrived(1)
    dx_arrived(2)
    for i in range(3):
        dx_copy(i).wait_send()
        du_copy(i).wait_send()
    du_copy(3).wait_send()
    dx_local.wait()
    for n in range(3):
        other = k.g_out.at[n, other_half]
        remote(other, other, k.gf_ss.at[n], k.gf_rs.at[n], dev_s).wait_recv()
        gf_copy(n).wait_send()
        gf_local(n).wait()
        for i in range(2):
            g1_copy(n, i).wait_send()
        g2_copy(n).wait_send()
        for bit in range(dp_bits):
            ga_copy(n, bit).wait_send()
    for i in range(len(rounds)):
        v_copy(i).wait_send()


def run_layer(mesh_sizes, args):
    tp_n, dp_n, dq_n = mesh_sizes
    lens, dom, cnt, x_in, wqkv_in, wo_in, wu_in, wd_in, queue_in, bias_in, vec_in, pos_in = args
    width = x_in.shape[1]
    crops_dev = lens.shape[0] // tp_n
    tokens = x_in.shape[0] // tp_n
    seq = tokens // crops_dev
    groups = dp_n * dq_n
    half = width // 2
    dp_bits = dp_n.bit_length() - 1
    hi_bits = (dq_n // 2).bit_length() - 1
    n_rounds = 1 + 2 + dp_bits + hi_bits
    heads = width // HD
    smem = pl.BlockSpec(memory_space=pltpu.SMEM)
    vmem = pl.BlockSpec(memory_space=pltpu.VMEM)
    hbm = pl.BlockSpec(memory_space=pl.ANY)
    dma = pltpu.SemaphoreType.DMA

    def b16(*shape):
        return pltpu.VMEM(shape, BF)

    def f32(*shape):
        return pltpu.VMEM(shape, F32)

    scratch = [
        b16(3, width, width),
        b16(width, width),
        b16(tp_n, width, width),
        b16(tp_n, width, width),
        b16(tokens, width),
        b16(3, tokens, width),
        b16(crops_dev * heads, seq, seq),
        b16(tokens, width),
        f32(tokens, width),
        f32(tokens, 1),
        b16(tokens, width),
        b16(tp_n, tokens, width),
        b16(tp_n, tokens, width),
        f32(tokens, width),
        f32(tokens, 1),
        b16(tokens, half),
        b16(tokens, width),
        b16(tokens, width),
        b16(tp_n, tokens, half),
        b16(tokens, width),
        b16(tp_n, tokens, half),
        b16(tokens, half),
        b16(3, tokens, width),
        b16(tokens, width),
        b16(tp_n, tokens, width),
        b16(tokens, width),
        b16(tokens, width),
        b16(tp_n, half, width),
        b16(3, 2, half, width),
        b16(3, half, width),
        b16(3, half, width),
        b16(3, max(hi_bits, 1), half // dp_n, width),
        b16(3, half, width),
        f32(tp_n, 8, width),
        f32(groups, 8, width),
        f32(64, tp_n * tokens),
        b16(128, tp_n * tokens),
        f32(groups, 8, width + 128),
        f32(groups, 8, width + 128),
        f32(8, width),
        f32(n_rounds + 1, 16, width),
        f32(n_rounds, 16, width),
        dma((7 + tp_n,)),
        dma((6, 3)),
        dma((6, 3)),
        dma((6, 3)),
        dma((6, tp_n)),
        dma((3, dp_n)),
        dma((3, dp_n)),
        dma((3,)),
        dma((3,)),
        dma((16,)),
        dma((16,)),
        dma((groups,)),
        dma((groups,)),
        dma((groups,)),
        dma((groups,)),
        dma((3, 2)),
        dma((3, 2)),
        dma((3,)),
        dma((3,)),
        dma((3, dp_bits)),
        dma((3, dp_bits)),
        dma((3, dp_bits)),
        dma((3, dp_bits)),
        dma((3, max(hi_bits, 1))),
        dma((3, max(hi_bits, 1))),
        dma((3,)),
        dma((3,)),
        dma((3,)),
        dma((3,)),
        dma((n_rounds,)),
        dma((n_rounds,)),
        dma((4,)),
    ]
    return pl.pallas_call(
        functools.partial(layer_kernel, (tp_n, dp_n, dq_n, crops_dev, seq, width)),
        out_shape=(
            jax.ShapeDtypeStruct((3, width, width), BF),
            jax.ShapeDtypeStruct((tp_n * tokens, width), BF),
            jax.ShapeDtypeStruct((16, width), F32),
        ),
        in_specs=[smem, smem, smem] + [hbm] * 6 + [vmem] * 3,
        out_specs=(hbm, hbm, vmem),
        scratch_shapes=scratch,
        compiler_params=pltpu.CompilerParams(
            collective_id=0, has_side_effects=True, vmem_limit_bytes=63 * 2**20
        ),
    )(*args)


def body(
    mesh_sizes,
    inputs,
    token_ids,
    crop_counts,
    domain_ids,
    positives,
    distractor_buffer,
    w_query,
    b_query,
    w_key,
    w_value,
    b_value,
    w_out,
    b_out,
    gain_one,
    shift_one,
    w_up,
    b_up,
    w_down,
    b_down,
    gain_two,
    shift_two,
):
    tp_n = mesh_sizes[0]
    tp = lax.axis_index("tp")
    width = inputs.shape[1]
    heads_w = w_query.shape[1]
    half = width // 2
    crops_dev = token_ids.shape[0] // tp_n
    lens = jnp.sum((token_ids != 0).astype(jnp.int32), axis=1)
    wqkv = jnp.stack([w_query.T, w_key.T, w_value.T])

    def placed(shard):
        return lax.dynamic_update_slice(jnp.zeros((width,), F32), shard, (tp * heads_w,))

    zero = jnp.zeros((width,), F32)
    bias_rows = jnp.stack([b_up, placed(b_query), placed(b_value)] + [zero] * 5)
    vec_rows = jnp.stack([b_out, gain_one, shift_one, b_down, gain_two, shift_two, zero, zero])
    own_positives = lax.dynamic_slice_in_dim(positives, tp * crops_dev, crops_dev).astype(F32)
    own_positives = jnp.pad(own_positives, ((0, 8 - crops_dev), (0, 0)))
    grads, dx, vec = run_layer(
        mesh_sizes,
        (
            lens,
            domain_ids,
            crop_counts,
            inputs,
            wqkv,
            w_out,
            w_up,
            w_down,
            distractor_buffer,
            bias_rows,
            vec_rows,
            own_positives,
        ),
    )
    grads = grads.astype(F32)
    grad_w_down = grads[0]
    grad_w_up = grads[1].reshape(2, half, 2, half).transpose(2, 1, 0, 3).reshape(width, width)
    heads = grads[2].reshape(2, 2, heads_w, 2, half)

    def untransposed(piece):
        return piece.transpose(0, 2, 1).reshape(width, heads_w)

    grad_w_query = untransposed(heads[:, 0, :, 0, :])
    grad_w_key = untransposed(heads[:, 0, :, 1, :])
    grad_w_value = untransposed(heads[:, 1, :, 0, :])
    grad_w_out = heads[:, 1, :, 1, :].transpose(1, 0, 2).reshape(heads_w, width)

    def own(row):
        return lax.dynamic_slice_in_dim(row, tp * heads_w, heads_w)

    return (
        dx.astype(F32),
        grad_w_query,
        own(vec[0]),
        grad_w_key,
        grad_w_value,
        own(vec[1]),
        grad_w_out,
        vec[2],
        vec[4],
        vec[5],
        grad_w_up,
        lax.dynamic_slice_in_dim(vec, 8 + tp, 1)[0],
        grad_w_down,
        vec[3],
        vec[6],
        vec[7],
    )


def solution(mesh):
    mesh_sizes = (mesh.shape["tp"], mesh.shape["dp"], mesh.shape["dq"])
    rows = P(("dp", "dq"), None)
    groups = P(("dp", "dq"))
    return jax.shard_map(
        functools.partial(body, mesh_sizes),
        mesh=mesh,
        in_specs=(
            rows,
            rows,
            groups,
            groups,
            rows,
            rows,
            P(None, "tp"),
            P("tp"),
            P(None, "tp"),
            P(None, "tp"),
            P("tp"),
            P("tp", None),
            P(),
            P(),
            P(),
            P(None, "tp"),
            P("tp"),
            P("tp", None),
            P(),
            P(),
            P(),
        ),
        out_specs=(
            rows,
            P(None, "tp"),
            P("tp"),
            P(None, "tp"),
            P(None, "tp"),
            P("tp"),
            P("tp", None),
            P(),
            P(),
            P(),
            P(None, "tp"),
            P("tp"),
            P("tp", None),
            P(),
            P(),
            P(),
        ),
        check_vma=False,
    )
```

time: 1120 us -> 274 us (0.24)
  waiting for transfers between devices: 805 us -> 0 us
  Pallas kernels: 0 us -> 231 us
  matrix products: 120 us -> 0 us
  blocking collectives: 73.5 us -> 0 us
  other arithmetic: 71 us -> 7.86 us
  between operations: 16.9 us -> 1.44 us
    psum x4 -> x0, waiting for transfers between devices: 521 us -> none  [the longest x2 278 us: forward(): attn_out = lax.psum(attn_partial, 'tp') + b_out]
    pallas_call x0 -> x1, Pallas kernels: none -> 231 us  [run_layer(): pl.pallas_call(functools.partial(layer_kernel, (tp_n, dp_n, dq_n, crops_d...]
    reduce_scatter x3 -> x0, waiting for transfers between devices: 167 us -> none  [the longest x2 141 us: share_sum(): lax.psum_scatter(partial_grad, 'tp', scatter_dimension=0, tiled=True)]
    dot_general x33 -> x0, matrix products: 120 us -> none  [the longest x1 22.7 us: forward(): ffn_partial = jnp.dot(active, w_down, preferred_element_type=jnp.float32)]
    all_gather x2 -> x0, waiting for transfers between devices: 117 us -> none  [share_sum(): return lax.all_gather(owned, 'tp', axis=0, tiled=True)]
    reduce_sum x22 -> x1, other arithmetic: 59.9 us -> 1.32 us  [body(): lens = jnp.sum((token_ids != 0).astype(jnp.int32), axis=1)]
    psum x1 -> x0, blocking collectives: 30.6 us -> none  [body(): lax.psum((grad_w_query, grad_b_query, grad_w_key, grad_w_value, grad_b_va...]
    all_gather x2 -> x0, blocking collectives: 26.2 us -> none  [the longest x1 14 us: body(): lax.all_gather(embedded_reduced, ('dp', 'dq'), axis=0, tiled=True)]
  transfers between devices with their start and end apart: 9 -> 0, of which waited for: 9 -> 0; matrix products, arithmetic and copies ran while one was open for 3% -> 0% of each run, Pallas kernels for 0% -> 0%
where the time goes in v1:
time: 274 us; the launch traced here: 273 us
  Pallas kernels  231 us (84%)
  local copies, waits for them, and re-layouts  32.8 us (12%)
  other arithmetic  7.86 us (3%)
    pallas_call x1, Pallas kernels, run_layer(): pl.pallas_call(functools.partial(layer_kernel, (tp_n, dp_n, dq_n, crops_d...  231 us

profile of v1, /device:TPU:0, one launch (start us, length us, event | category | flops | bytes accessed | tf_op | source)
XLA Modules:
  0.0 272.8 jit_solution(14488022581120220673)
XLA Ops:
  0.7 0.8 dynamic_update_slice.8
  1.5 0.8 dynamic_update_slice.9
  2.3 0.7 stack.57
  3.0 0.6 stack.62.refs_9_
  3.6 0.6 pad_convert_fusion.refs_11_
  4.2 2.1 pad_maximum_fusion.refs_4_
  6.4 0.7 stack.63
  7.1 0.7 stack.64
  7.8 0.7 stack.65
  8.5 0.7 stack.66
  9.2 0.7 stack.67
  9.8 0.7 stack.68
  10.5 0.6 stack.70.refs_10_
  11.2 1.3 convert_reduce_fusion.refs_0_
  13.2 230.8 %shard_map.324 = (bf16[3,768,768]{2,1,0:T(8,128)(2,1)}, bf16[2048,768]{1,0:T(8,128)(2,1)}, f32[16,768]{1,0:T(8,128)}) custom-call(s32[8]{0:T(128)} %convert_reduce_fusion.refs_0_, s32[8]{0:T(128)} %refs_1_.1, s32[1]{0:T(128)S(6)} %copy.57.refs_2_, bf16[2048,768]{1,0:T(8,128)(2,1)} %refs_3_.1, bf16[3,192,768]{2,1,0:T(8,128)(2,1)} %pad_maximum_fusion.refs_4_, ...), custom_call_target="tpu_custom_call" | custom-call | tf_op jit(solution)/shard_map/pallas_call | solution.py:1052
  243.9 1.7 slice_reduce_fusion
  245.6 0.6 constant_dynamic-slice_fusion
  246.3 4.2 %fusion = (f32[1,768,768]{2,1,0:T(8,128)}, f32[1,768,768]{2,1,0:T(8,128)}) fusion(bf16[3,768,768]{2,1,0:T(8,128)(2,1)} %get-tuple-element.20), kind=kLoop, calls=%fused_computation.18 | loop fusion | bytes 9437184 | tf_op jit(solution)/shard_map/slice | solution.py:1128
  250.4 2.9 %reshape_squeeze.6 = f32[2,2,192,2,384]{4,3,2,1,0:T(2,128)S(1)} reshape(f32[1,768,768]{2,1,0:T(8,128)} %get-tuple-element.30) | data formatting | bytes 4718592 | tf_op jit(solution)/shard_map/reshape;squeeze | solution.py:1129
  253.4 1.7 fusion.1
  255.2 0.9 copy.48
  256.0 0.9 copy.49
  257.0 0.9 copy.46
  257.8 0.9 copy.47
  258.7 2.9 %reshape_squeeze.7 = f32[2,384,2,384]{3,2,1,0:T(2,128)S(1)} reshape(f32[1,768,768]{2,1,0:T(8,128)} %get-tuple-element.29) | data formatting | bytes 4718592 | tf_op jit(solution)/shard_map/reshape;squeeze | solution.py:1128
  261.6 1.8 copy.41
  263.4 1.6 copy.50
  265.0 1.3 copy-done.1
  266.3 0.6 convert_element_type.14
  266.9 1.6 slice_bitcast_fusion
  268.5 1.2 copy-done.2
  269.6 3.2 %convert_element_type.13 = f32[2048,768]{1,0:T(8,128)} convert(bf16[2048,768]{1,0:T(8,128)(2,1)S(1)} %copy-done.2) | non-fusion elementwise | flops 1572864 | bytes 9437184 | tf_op jit(solution)/shard_map/convert_element_type | solution.py:1143
  (12 shorter events, 0.2 us)
Async XLA Ops:
  0.6 3.0 %copy-start = (bf16[8,768]{1,0:T(8,128)(2,1)S(1)}, bf16[8,768]{1,0:T(8,128)(2,1)}, u32[]{:S(2)}) copy-start(bf16[8,768]{1,0:T(8,128)(2,1)} %param.25) | copy-start | bytes 36868
  263.4 2.9 %copy-start.1 = (bf16[3,768,768]{2,1,0:T(8,128)(2,1)S(1)}, bf16[3,768,768]{2,1,0:T(8,128)(2,1)}, u32[]{:S(2)}) copy-start(bf16[3,768,768]{2,1,0:T(8,128)(2,1)} %get-tuple-element.20) | copy-start | bytes 10616836
  266.9 2.7 %copy-start.2 = (bf16[2048,768]{1,0:T(8,128)(2,1)S(1)}, bf16[2048,768]{1,0:T(8,128)(2,1)}, u32[]{:S(2)}) copy-start(bf16[2048,768]{1,0:T(8,128)(2,1)} %get-tuple-element.19) | copy-start | bytes 9437188
